TPU v7x, 32 devices: a whole 2x2x4 slice. The times are simulated.
32 devices in a mesh: rows: 8 (over z, x), cols: 4 (over y, core).
Axes of the slice: x: 2, y: 2, z: 4, core: 2. Of those that a mesh axis runs over, the one named last changes fastest.
Arguments:
- doc_tiles: bfloat16 [8, 4, 46, 512, 512], P('rows', 'cols'), may hold values from -0.15625 to 0.15625
- tile_rows: int32 [8, 4, 46], P('rows', 'cols'), may hold values from 0 to 7
- tile_cols: int32 [8, 4, 46], P('rows', 'cols'), may hold values from 0 to 95, as said below
- counts: int32 [8, 4], P('rows', 'cols'), may hold values from 23 to 46, as said below
- start_block: bfloat16 [32768, 128], P(('rows', 'cols')), may hold values from -6 to 6
Outputs:
- basis: float32 [32768, 128], P(('rows', 'cols'))
- factor: float32 [128, 128], replicated
Inputs may be any that keep to these rules, and one draw needn't show every extreme that they name: `tile_cols`: A term block index c of term group j is owned by the device of rows index c // 12. On each device at most 6 slots name term blocks of one owner, and some owner is named by exactly 6 slots. `counts`: some device has all 46 slots live.
All inputs are finite; a program needn't handle non-finite values.
Results may differ from a plain program's by a relative error of at most 0.002.
Values may be sent and summed in bfloat16 or wider, within the bound.
A program may use at most 128 MiB of HBM per device.

v0:
```python
import jax
import jax.numpy as jnp
from jax import lax
from jax.sharding import PartitionSpec as P

RB = 8
CB_DEV = 12


def local(doc_tiles, tile_rows, tile_cols, counts, start_block):
    tiles_here = doc_tiles[0, 0]
    rows_here = tile_rows[0, 0]
    cols_here = tile_cols[0, 0]
    slots = tiles_here.shape[0]
    width = tiles_here.shape[1]
    vectors = start_block.shape[1]
    groups = lax.axis_size("rows")
    per_owner = (slots + groups - 1) // groups
    buffer_slots = groups * per_owner
    slot_index = jnp.arange(slots, dtype=jnp.int32)
    alive = (slot_index < counts[0, 0]).astype(jnp.float32)
    owner_of = cols_here // CB_DEV
    inside_range = cols_here % CB_DEV
    earlier = (owner_of[:, None] == owner_of[None, :]) & (slot_index[None, :] < slot_index[:, None])
    target = owner_of * per_owner + jnp.sum(earlier.astype(jnp.int32), axis=1)
    selector = (jnp.arange(buffer_slots, dtype=jnp.int32)[:, None] == target[None, :]).astype(
        jnp.bfloat16
    )
    group_docs = lax.all_gather(start_block, "cols", axis=0, tiled=True)
    document_block_list = group_docs.reshape(RB, width, vectors)
    picked = jnp.take(document_block_list, rows_here, axis=0)
    tile_terms = jnp.einsum("sqp,sqk->spk", tiles_here, picked, preferred_element_type=jnp.float32)
    tile_terms = (tile_terms * alive[:, None, None]).astype(jnp.bfloat16)
    outgoing = jnp.einsum(
        "cs,spk->cpk", selector, tile_terms, preferred_element_type=jnp.float32
    ).astype(jnp.bfloat16)
    outgoing = outgoing.reshape(groups, per_owner, width, vectors)
    labelled_row_set = (
        inside_range[:, None] == jnp.arange(CB_DEV, dtype=jnp.int32)[None, :]
    ).astype(jnp.float32) * alive[:, None]
    label_array = jnp.dot(
        selector, labelled_row_set.astype(jnp.bfloat16), preferred_element_type=jnp.float32
    ).astype(jnp.bfloat16)
    label_array = label_array.reshape(groups, per_owner, CB_DEV)
    arrived, arrived_labels = (
        lax.all_to_all(outgoing, "rows", split_axis=0, concat_axis=0, tiled=True),
        lax.all_to_all(label_array, "rows", split_axis=0, concat_axis=0, tiled=True),
    )
    owned = jnp.einsum(
        "scl,scpk->lpk", arrived_labels, arrived, preferred_element_type=jnp.float32
    ).astype(jnp.bfloat16)
    every_block = lax.all_gather(owned, "rows", axis=0, tiled=True)
    wanted = jnp.take(every_block, cols_here, axis=0)
    product_terms = jnp.einsum(
        "sqp,spk->sqk", tiles_here, wanted, preferred_element_type=jnp.float32
    )
    product_terms = product_terms * alive[:, None, None]
    row_match_flags = (rows_here[:, None] == jnp.arange(RB, dtype=jnp.int32)[None, :]).astype(
        jnp.float32
    )
    partial_row_set = jnp.einsum(
        "nf,nlj->flj", row_match_flags, product_terms, precision=lax.Precision.HIGHEST
    )
    partial_row_set = partial_row_set.reshape(RB * width, vectors)
    own_rows = lax.psum_scatter(partial_row_set, "cols", scatter_dimension=0, tiled=True)
    total_docs = own_rows.shape[0] * lax.axis_size("rows") * lax.axis_size("cols")
    local_gram = jnp.dot(
        own_rows.T, own_rows, precision=lax.Precision.HIGHEST, preferred_element_type=jnp.float32
    )
    gram_total = lax.psum(local_gram, ("rows", "cols")) / total_docs
    lower_factor = jnp.linalg.cholesky(gram_total)
    basis = lax.linalg.triangular_solve(
        lower_factor, own_rows, left_side=False, lower=True, transpose_a=True
    )
    return (basis, lower_factor.T)


def solution(mesh):
    placed = (
        P("rows", "cols", None, None, None),
        P("rows", "cols", None),
        P("rows", "cols", None),
        P("rows", "cols"),
        P(("rows", "cols"), None),
    )
    return jax.shard_map(
        local,
        mesh=mesh,
        in_specs=placed,
        out_specs=(P(("rows", "cols"), None), P()),
        check_vma=False,
    )
```

profile of v0, /device:TPU:0, one launch (start us, length us, event | category | flops | bytes accessed | tf_op | source)
XLA Modules:
  0.0 632.0 jit_solution(2493299129950930785)
XLA Ops:
  7.2 0.7 all-gather.3.cloned.1.call-update
  8.5 0.7 and_select_fusion
  9.4 0.7 compare_and_fusion
  10.4 0.6 reshape.158
  11.1 7.3 %all-to-all-start = ((bf16[8,6,12]{2,1,0:T(8,128)(2,1)}), bf16[8,6,12]{2,1,0:T(8,128)(2,1)S(1)}, u32[]{:S(2)}, u32[]{:S(2)}) async-start(bf16[8,6,12]{2,1,0:T(8,128)(2,1)} %reshape.158), calls=%async_computation | async-start | bytes 32768 | tf_op jit(solution)/shard_map/all_to_all | solution.py:47
  18.4 0.7 fusion.40
  19.0 10.0 %all-gather.3.cloned.1.call-done = bf16[4096,128]{1,0:T(8,128)(2,1)} async-done(((bf16[1024,128]{1,0:T(8,128)(2,1)}), bf16[4096,128]{1,0:T(8,128)(2,1)}) %all-gather.3.cloned.1.call-update) | async-done | bytes 1048592 | tf_op jit(solution)/shard_map/all_gather | solution.py:29
  29.1 6.1 gather_fusion
  35.1 14.7 %fusion.6 = bf16[46,512,128]{1,2,0:T(8,128)(2,1)} fusion(f32[46]{0:T(128)S(1)} %get-tuple-element.17, bf16[1,1,46,512,512]{4,3,2,1,0:T(8,128)(2,1)} %param.5, bf16[46,512,128]{2,1,0:T(8,128)(2,1)} %gather_fusion, pred[46]{0:T(512)(128)(4,1)S(1)} %get-tuple-element.16), kind=kOutput, calls=%fused_computation.10 | convolution fusion | flops 3096051712 | bytes 36176104 | tf_op jit(solution)/shard_map/sqp,sqk->spk/dot_general | solution.py:32
  49.9 9.0 %copy.42 = bf16[46,512,128]{2,0,1:T(8,128)(2,1)} copy(bf16[46,512,128]{1,2,0:T(8,128)(2,1)} %fusion.6) | data formatting | bytes 12058624 | tf_op jit(solution)/shard_map/convert_element_type | solution.py:33
  58.8 4.5 convolution_convert_fusion
  63.4 4.3 copy.43
  67.7 144.0 %all_to_all.10 = bf16[8,6,512,128]{3,2,1,0:T(8,128)(2,1)S(1)} all-to-all(bf16[8,6,512,128]{3,2,1,0:T(8,128)(2,1)} %bitcast.68), channel_id=1, replica_groups=mesh['rows'=8,'cols'=4] {'rows'}, dimensions={0} | all-to-all | bytes 12582912 | tf_op jit(solution)/shard_map/all_to_all | solution.py:46
  211.6 6.9 %bitcast_convert_fusion = bf16[12,512,128]{2,0,1:T(8,128)(2,1)S(1)} fusion(bf16[8,6,512,128]{3,2,1,0:T(8,128)(2,1)S(1)} %all_to_all.10, bf16[8,6,12]{2,1,0:T(8,128)(2,1)S(1)} %all-to-all-done), kind=kOutput, calls=%fused_computation.15 | convolution fusion | flops 76283904 | bytes 7865472 | tf_op jit(solution)/shard_map/scl,scpk->lpk/dot_general | solution.py:49
  218.5 1.6 copy.45
  220.4 174.4 %all-gather.5.cloned.1.call-done = bf16[96,512,128]{2,1,0:T(8,128)(2,1)} async-done(((bf16[12,512,128]{2,1,0:T(8,128)(2,1)}), bf16[96,512,128]{2,1,0:T(8,128)(2,1)}) %all-gather.5.cloned.1.call-update) | async-done | bytes 12582928 | tf_op jit(solution)/shard_map/all_gather | solution.py:52
  394.8 9.4 %gather_fusion.1 = bf16[46,512,128]{2,1,0:T(8,128)(2,1)} fusion(bf16[96,512,128]{2,1,0:T(8,128)(2,1)} %all-gather.5.cloned.1.call-done, s32[1024]{0:T(1024)S(1)} %pad_clamp_fusion), kind=kCustom, calls=%fused_computation.1 | custom fusion | bytes 12058808 | tf_op jit(solution)/shard_map/jit(_take)/gather | solution.py:53
  404.2 17.6 %multiply_bitcast_fusion = f32[46,512,128]{1,2,0:T(8,128)} fusion(f32[46]{0:T(128)S(1)} %get-tuple-element.17, bf16[1,1,46,512,512]{4,3,2,1,0:T(8,128)(2,1)} %param.5, bf16[46,512,128]{2,1,0:T(8,128)(2,1)} %gather_fusion.1, pred[46]{0:T(512)(128)(4,1)S(1)} %compare_and_fusion.1), kind=kOutput, calls=%fused_computation.6 | convolution fusion | flops 3093037056 | bytes 42205416 | tf_op jit(solution)/shard_map/sqp,spk->sqk/dot_general | solution.py:54
  421.8 12.6 %copy.47 = f32[46,512,128]{2,0,1:T(8,128)} copy(f32[46,512,128]{1,2,0:T(8,128)} %multiply_bitcast_fusion) | data formatting | bytes 24117248 | tf_op jit(solution)/shard_map/mul | solution.py:57
  434.5 7.1 %fusion.37 = f32[8,512,128]{2,0,1:T(8,128)S(1)} fusion(f32[46,512,128]{2,0,1:T(8,128)} %copy.47, s32[46]{0:T(128)S(1)} %bitcast.70), kind=kOutput, calls=%fused_computation.48 | convolution fusion | flops 289407360 | bytes 14155960 | tf_op jit(solution)/shard_map/nf,nlj->flj/dot_general | solution.py:61
  441.6 1.7 copy.48
  443.7 29.4 %reduce-scatter.2.cloned.1.call-done = f32[1024,128]{1,0:T(8,128)} async-done(((f32[4096,128]{1,0:T(8,128)}), f32[1024,128]{1,0:T(8,128)}) %reduce-scatter.2.cloned.1.call-update) | async-done | bytes 524304 | tf_op jit(solution)/shard_map/reduce_scatter | solution.py:65
  473.1 2.8 fusion.45
  476.0 121.7 %all-reduce.2.cloned.1.call-done = f32[128,128]{0,1:T(8,128)} async-done(((f32[128,128]{0,1:T(8,128)}), f32[128,128]{0,1:T(8,128)}) %all-reduce.2.cloned.1.call-update) | async-done | bytes 65552 | tf_op jit(solution)/shard_map/psum | solution.py:70
  597.6 0.8 broadcast_multiply_fusion
  598.6 0.9 fusion.25
  599.4 11.7 %cholesky.16 = f32[128,128]{1,0:T(8,128)S(1)} custom-call(f32[128,128]{1,0:T(8,128)S(1)} %fusion.25), custom_call_target="Cholesky" | custom-call | tf_op jit(solution)/shard_map/jit(cholesky)/cholesky | solution.py:71
  611.2 0.6 compare_reduce_fusion
  611.8 0.7 fusion.26
  612.5 0.7 copy.51
  613.2 9.8 %custom-call.6 = f32[1,128,128]{1,2,0:T(8,128)S(1)} custom-call(f32[1,128,128]{2,1,0:T(8,128)S(1)} %get-tuple-element.13), custom_call_target="InvertDiagBlocksLowerTriangular" | custom-call | tf_op jit(solution)/shard_map/triangular_solve | solution.py:72
  623.0 2.4 fusion.23
  (22 shorter events, 1.4 us)
Async XLA Ops:
  7.2 21.9 %all-gather.3.cloned.1.call-start = ((), (), s32[]{:S(2)}) async-start(), calls=%async_computation.3 | async-start | bytes 1310720 | tf_op jit(solution)/shard_map/all_gather | solution.py:29
  11.1 56.6 %all-to-all-start = ((bf16[8,6,12]{2,1,0:T(8,128)(2,1)}), bf16[8,6,12]{2,1,0:T(8,128)(2,1)S(1)}, u32[]{:S(2)}, u32[]{:S(2)}) async-start(bf16[8,6,12]{2,1,0:T(8,128)(2,1)} %reshape.158), calls=%async_computation | async-start | bytes 32768 | tf_op jit(solution)/shard_map/all_to_all | solution.py:47
  18.3 376.5 %all-gather.5.cloned.1.call-start = ((), (), s32[]{:S(2)}) async-start(), calls=%async_computation.4 | async-start | bytes 14155776 | tf_op jit(solution)/shard_map/all_gather | solution.py:52
  211.6 8.8 %copy-start.1 = (s32[1,1,46]{2,1,0:T(1,128)S(1)}, s32[1,1,46]{2,1,0:T(1,128)}, u32[]{:S(2)}) copy-start(s32[1,1,46]{2,1,0:T(1,128)} %param.7) | copy-start | bytes 556
  220.1 253.0 %reduce-scatter.2.cloned.1.call-start = ((), (), s32[]{:S(2)}) async-start(), calls=%async_computation.5 | async-start | bytes 2621440 | tf_op jit(solution)/shard_map/reduce_scatter | solution.py:65
  421.8 12.6 %copy-start = (s32[1,1,46]{2,1,0:T(1,128)S(1)}, s32[1,1,46]{2,1,0:T(1,128)}, u32[]{:S(2)}) copy-start(s32[1,1,46]{2,1,0:T(1,128)} %param.6) | copy-start | bytes 556
  443.4 154.3 %all-reduce.2.cloned.1.call-start = ((), (), s32[]{:S(2)}) async-start(), calls=%async_computation.6 | async-start | bytes 131072 | tf_op jit(solution)/shard_map/psum | solution.py:70
Sparse Core Ops, SparseCore 0:
  9.6 19.4 all-gather.2
  220.3 174.5 all-gather.4
  443.5 29.5 reduce-scatter.1
  480.1 117.5 all-reduce.1
where the time goes:
time: 634 us; the launch traced here: 632 us
  waiting for transfers between devices  336 us (53%)
  blocking collectives  144 us (23%)
  matrix products  56.3 us (9%)
  local copies, waits for them, and re-layouts  46.2 us (7%)
  other arithmetic  26.8 us (4%)
  between operations  14.5 us (2%)
  starting transfers between devices  7.89 us (1%)
    all_gather x1, waiting for transfers between devices, local(): every_block = lax.all_gather(owned, 'rows', axis=0, tiled=True)  174 us
    all_to_all x1, blocking collectives, local(): lax.all_to_all(outgoing, 'rows', split_axis=0, concat_axis=0, tiled=True)  144 us
    psum x1, waiting for transfers between devices, local(): gram_total = lax.psum(local_gram, ('rows', 'cols')) / total_docs  122 us
    reduce_scatter x1, waiting for transfers between devices, local(): lax.psum_scatter(partial_row_set, 'cols', scatter_dimension=0, tiled=True)  29.4 us
    dot_general x1, matrix products, local(): jnp.einsum('sqp,spk->sqk', tiles_here, wanted, preferred_element_type=jnp...  17.6 us
    dot_general x1, matrix products, local(): jnp.einsum('sqp,sqk->spk', tiles_here, picked, preferred_element_type=jnp...  14.7 us
  transfers between devices with their start and end apart: 5, of which 4 were waited for; matrix products, arithmetic and copies ran while one was open for 7% of the time, Pallas kernels for 0%

commit v1 on v0

v1 whole, which is shorter than its diff:
```python
import functools

import jax
import jax.numpy as jnp
from jax import lax
from jax.experimental import pallas as pl
from jax.experimental.pallas import tpu as pltpu
from jax.sharding import PartitionSpec as P

RB = 8
CB_DEV = 12
MESH = pl.DeviceIdType.MESH
MIB = 1024 * 1024


def terms_kernel(per_owner, order_ref, row_ref, live_ref, docs_ref, *rest):
    tile_refs, out_ref = rest[:per_owner], rest[per_owner]
    step = pl.program_id(0)
    for c in range(per_owner):
        at = step * per_owner + c
        term = jnp.dot(
            docs_ref[row_ref[at]], tile_refs[c][0], preferred_element_type=jnp.float32
        )
        out_ref[c] = jnp.where(live_ref[at] > 0, term, 0.0).astype(out_ref.dtype)


def terms_call(order, row, live, docs, tiles, groups, per_owner):
    _, width, _ = tiles.shape
    vectors = docs.shape[1]
    tile_specs = [
        pl.BlockSpec(
            (1, width, width), lambda i, o, r, v, c=c: (o[i * per_owner + c], 0, 0)
        )
        for c in range(per_owner)
    ]
    return pl.pallas_call(
        functools.partial(terms_kernel, per_owner),
        grid_spec=pltpu.PrefetchScalarGridSpec(
            num_scalar_prefetch=3,
            grid=(groups,),
            in_specs=[pl.BlockSpec((RB, vectors, width), lambda i, o, r, v: (0, 0, 0))]
            + tile_specs,
            out_specs=pl.BlockSpec((per_owner, vectors, width), lambda i, o, r, v: (i, 0, 0)),
        ),
        out_shape=jax.ShapeDtypeStruct((groups * per_owner, vectors, width), jnp.bfloat16),
        compiler_params=pltpu.CompilerParams(vmem_limit_bytes=40 * MIB),
        name="terms",
    )(order, row, live, docs, *([tiles] * per_owner))


def combine_kernel(per_owner, groups, label_ref, arrived_ref, out_ref, owned):
    step = pl.program_id(0)

    @pl.when(step == 0)
    def _():
        owned[...] = jnp.zeros_like(owned)

    @pl.when(step < groups)
    def _():
        for c in range(per_owner):
            label = label_ref[step * per_owner + c]
            at = jnp.maximum(label, 0)

            @pl.when(label >= 0)
            def _():
                owned[at] = owned[at] + arrived_ref[c].astype(jnp.float32)

    @pl.when(step >= groups)
    def _():
        for c in range(per_owner):
            label = label_ref[(step - groups) * per_owner + c]
            out_ref[c] = owned[jnp.maximum(label, 0)].astype(out_ref.dtype)


def combine_call(labels, arrived, groups, per_owner):
    _, vectors, width = arrived.shape
    return pl.pallas_call(
        functools.partial(combine_kernel, per_owner, groups),
        grid_spec=pltpu.PrefetchScalarGridSpec(
            num_scalar_prefetch=1,
            grid=(2 * groups,),
            in_specs=[
                pl.BlockSpec(
                    (per_owner, vectors, width),
                    lambda i, l: (jnp.minimum(i, groups - 1), 0, 0),
                )
            ],
            out_specs=pl.BlockSpec(
                (per_owner, vectors, width), lambda i, l: (jnp.maximum(i - groups, 0), 0, 0)
            ),
            scratch_shapes=[pltpu.VMEM((CB_DEV, vectors, width), jnp.float32)],
        ),
        out_shape=jax.ShapeDtypeStruct(arrived.shape, jnp.bfloat16),
        compiler_params=pltpu.CompilerParams(vmem_limit_bytes=24 * MIB),
        name="combine",
    )(labels, arrived)


def sample_kernel(per_owner, order_ref, row_ref, live_ref, wanted_ref, *rest):
    tile_refs, out_ref = rest[:per_owner], rest[per_owner]
    step = pl.program_id(0)

    @pl.when(step == 0)
    def _():
        out_ref[...] = jnp.zeros_like(out_ref)

    for c in range(per_owner):
        at = step * per_owner + c
        row = row_ref[at]

        @pl.when(live_ref[at] > 0)
        def _():
            out_ref[row] = out_ref[row] + lax.dot_general(
                tile_refs[c][0],
                wanted_ref[c],
                (((1,), (1,)), ((), ())),
                preferred_element_type=jnp.float32,
            )


def sample_call(order, row, live, wanted, tiles, groups, per_owner):
    _, width, _ = tiles.shape
    vectors = wanted.shape[1]
    tile_specs = [
        pl.BlockSpec(
            (1, width, width), lambda i, o, r, v, c=c: (o[i * per_owner + c], 0, 0)
        )
        for c in range(per_owner)
    ]
    return pl.pallas_call(
        functools.partial(sample_kernel, per_owner),
        grid_spec=pltpu.PrefetchScalarGridSpec(
            num_scalar_prefetch=3,
            grid=(groups,),
            in_specs=[pl.BlockSpec((per_owner, vectors, width), lambda i, o, r, v: (i, 0, 0))]
            + tile_specs,
            out_specs=pl.BlockSpec((RB, width, vectors), lambda i, o, r, v: (0, 0, 0)),
        ),
        out_shape=jax.ShapeDtypeStruct((RB, width, vectors), jnp.float32),
        compiler_params=pltpu.CompilerParams(vmem_limit_bytes=40 * MIB),
        name="sample",
    )(order, row, live, wanted, *([tiles] * per_owner))


def sum_kernel(axes, x_ref, out_ref, arrived, send_sem, recv_sem):
    place = {name: lax.axis_index(name) for name, _ in axes}
    partners = []
    for name, size in axes:
        bit = 1
        while bit < size:
            other = dict(place)
            mine = place[name]
            other[name] = jnp.where((mine // bit) % 2 == 0, mine + bit, mine - bit)
            partners.append((other["rows"], other["cols"]))
            bit *= 2
    barrier = pltpu.get_barrier_semaphore()
    for partner in partners:
        pl.semaphore_signal(barrier, inc=1, device_id=partner, device_id_type=MESH)
    pl.semaphore_wait(barrier, len(partners))
    for step, partner in enumerate(partners):
        source = x_ref if step == 0 else out_ref.at[step - 1]
        copy = pltpu.make_async_remote_copy(
            src_ref=source,
            dst_ref=arrived.at[step],
            send_sem=send_sem.at[step],
            recv_sem=recv_sem.at[step],
            device_id=partner,
            device_id_type=MESH,
        )
        copy.start()
        copy.wait()
        out_ref[step] = source[...] + arrived[step]


def sum_everywhere(x):
    axes = [("cols", lax.axis_size("cols")), ("rows", lax.axis_size("rows"))]
    steps = sum(size.bit_length() - 1 for _, size in axes)
    shape = (steps,) + x.shape
    return pl.pallas_call(
        functools.partial(sum_kernel, axes),
        out_shape=jax.ShapeDtypeStruct(shape, x.dtype),
        in_specs=[pl.BlockSpec(memory_space=pltpu.VMEM)],
        out_specs=pl.BlockSpec(memory_space=pltpu.VMEM),
        scratch_shapes=[
            pltpu.VMEM(shape, x.dtype),
            pltpu.SemaphoreType.DMA((steps,)),
            pltpu.SemaphoreType.DMA((steps,)),
        ],
        compiler_params=pltpu.CompilerParams(collective_id=1, has_side_effects=True),
        name="gram_sum",
    )(x)[steps - 1]


def local(doc_tiles, tile_rows, tile_cols, counts, start_block):
    tiles = doc_tiles[0, 0]
    rows_here = tile_rows[0, 0]
    cols_here = tile_cols[0, 0]
    slots, width, _ = tiles.shape
    vectors = start_block.shape[1]
    groups = lax.axis_size("rows")
    per_owner = (slots + groups - 1) // groups
    places = groups * per_owner
    slot_index = jnp.arange(slots, dtype=jnp.int32)
    alive = (slot_index < counts[0, 0]).astype(jnp.int32)
    owner_of = cols_here // CB_DEV
    earlier = (owner_of[:, None] == owner_of[None, :]) & (slot_index[None, :] < slot_index[:, None])
    target = owner_of * per_owner + jnp.sum(earlier.astype(jnp.int32), axis=1)
    chosen = (jnp.arange(places, dtype=jnp.int32)[:, None] == target[None, :]).astype(jnp.int32)
    order = jnp.sum(chosen * slot_index[None, :], axis=1)
    row = jnp.sum(chosen * rows_here[None, :], axis=1)
    live = jnp.sum(chosen * alive[None, :], axis=1)
    label = jnp.sum(chosen * (alive * (cols_here % CB_DEV + 1))[None, :], axis=1) - 1
    labels = lax.all_to_all(
        label.reshape(groups, per_owner), "rows", split_axis=0, concat_axis=0, tiled=True
    ).reshape(places)
    group_docs = lax.all_gather(start_block, "cols", axis=0, tiled=True)
    docs = jnp.swapaxes(group_docs.reshape(RB, width, vectors), 1, 2)
    terms = terms_call(order, row, live, docs, tiles, groups, per_owner)

    def exchange(blocks):
        blocks = blocks.reshape(groups, per_owner, vectors, width)
        blocks = lax.all_to_all(blocks, "rows", split_axis=0, concat_axis=0, tiled=True)
        return blocks.reshape(places, vectors, width)

    wanted = exchange(combine_call(labels, exchange(terms), groups, per_owner))
    partial_rows = sample_call(order, row, live, wanted, tiles, groups, per_owner)
    partial_rows = partial_rows.reshape(RB * width, vectors)
    own_rows = lax.psum_scatter(partial_rows, "cols", scatter_dimension=0, tiled=True)
    total_docs = own_rows.shape[0] * lax.axis_size("rows") * lax.axis_size("cols")
    local_gram = jnp.dot(
        own_rows.T, own_rows, precision=lax.Precision.HIGHEST, preferred_element_type=jnp.float32
    )
    gram_total = sum_everywhere(local_gram) / total_docs
    lower_factor = jnp.linalg.cholesky(gram_total)
    basis = lax.linalg.triangular_solve(
        lower_factor, own_rows, left_side=False, lower=True, transpose_a=True
    )
    return (basis, lower_factor.T)


def solution(mesh):
    placed = (
        P("rows", "cols", None, None, None),
        P("rows", "cols", None),
        P("rows", "cols", None),
        P("rows", "cols"),
        P(("rows", "cols"), None),
    )
    return jax.shard_map(
        local,
        mesh=mesh,
        in_specs=placed,
        out_specs=(P(("rows", "cols"), None), P()),
        check_vma=False,
    )
```

time: 634 us -> 444 us (0.70)
  waiting for transfers between devices: 336 us -> 179 us
  Pallas kernels: 0 us -> 57.2 us
  matrix products: 56.3 us -> 5.23 us
  local copies, waits for them, and re-layouts: 46.2 us -> 7.15 us
    all_gather x1 -> x0, waiting for transfers between devices: 174 us -> none  [local(): every_block = lax.all_gather(owned, 'rows', axis=0, tiled=True)]
    all_to_all x1 -> x2, waiting for transfers between devices: 0.01 us -> 137 us  [the longest x1 137 us: exchange(): lax.all_to_all(blocks, 'rows', split_axis=0, concat_axis=0, tiled=True)]
    psum x1 -> x0, waiting for transfers between devices: 122 us -> none  [local(): gram_total = lax.psum(local_gram, ('rows', 'cols')) / total_docs]
    pallas_call x0 -> x4, Pallas kernels: none -> 57.2 us  [the longest x1 20 us: sum_everywhere(): pl.pallas_call(functools.partial(sum_kernel, axes), out_shape=jax.ShapeDt...]
    dot_general x6 -> x0, matrix products: 51.1 us -> none  [the longest x1 17.6 us: local(): jnp.einsum('sqp,spk->sqk', tiles_here, wanted, preferred_element_type=jnp...]
    gather x2 -> x0, local copies, waits for them, and re-layouts: 15.5 us -> none  [the longest x1 9.41 us: local(): wanted = jnp.take(every_block, cols_here, axis=0)]
    convert_element_type x4 -> x0, local copies, waits for them, and re-layouts: 14.9 us -> none  [the longest x1 8.96 us: local(): tile_terms = (tile_terms * alive[:, None, None]).astype(jnp.bfloat16)]
    mul x1 -> x0, local copies, waits for them, and re-layouts: 12.6 us -> none  [local(): product_terms = product_terms * alive[:, None, None]]
  transfers between devices with their start and end apart: 5 -> 4, of which waited for: 4 -> 3; matrix products, arithmetic and copies ran while one was open for 7% -> 1% of each run, Pallas kernels for 0% -> 3%
where the time goes in v1:
time: 444 us; the launch traced here: 443 us
  waiting for transfers between devices  179 us (40%)
  blocking collectives  142 us (32%)
  Pallas kernels  57.2 us (13%)
  other arithmetic  25.2 us (6%)
  between operations  14.8 us (3%)
  starting transfers between devices  12.8 us (3%)
  local copies, waits for them, and re-layouts  7.15 us (2%)
  matrix products  5.23 us (1%)
    all_to_all x1, blocking collectives, exchange(): lax.all_to_all(blocks, 'rows', split_axis=0, concat_axis=0, tiled=True)  142 us
    all_to_all x1, waiting for transfers between devices, exchange(): lax.all_to_all(blocks, 'rows', split_axis=0, concat_axis=0, tiled=True)  137 us
    reduce_scatter x1, waiting for transfers between devices, local(): lax.psum_scatter(partial_rows, 'cols', scatter_dimension=0, tiled=True)  29.7 us
    pallas_call x1, Pallas kernels, sum_everywhere(): pl.pallas_call(functools.partial(sum_kernel, axes), out_shape=jax.ShapeDt...  20 us
    pallas_call x1, Pallas kernels, sample_call(): pl.pallas_call(functools.partial(sample_kernel, per_owner), grid_spec=plt...  18.1 us
    another operation x3, other arithmetic, local(): lower_factor = jnp.linalg.cholesky(gram_total)  12.4 us
    pallas_call x1, Pallas kernels, terms_call(): pl.pallas_call(functools.partial(terms_kernel, per_owner), grid_spec=pltp...  12 us
    all_gather x1, waiting for transfers between devices, local(): group_docs = lax.all_gather(start_block, 'cols', axis=0, tiled=True)  10.9 us
  transfers between devices with their start and end apart: 4, of which 3 were waited for; matrix products, arithmetic and copies ran while one was open for 1% of the time, Pallas kernels for 3%

profile of v1, /device:TPU:0, one launch (start us, length us, event | category | flops | bytes accessed | tf_op | source)
XLA Modules:
  0.0 442.8 jit_solution(3242975667916999958)
XLA Ops:
  7.2 0.0 all-gather.2.cloned.1.call-start
  7.2 0.7 all-gather.2.cloned.1.call-update
  8.6 0.7 fusion.5
  9.2 0.2 convert_reduce_fusion
  9.4 0.8 select_reduce_fusion.1
  10.2 0.7 sub.14
  10.9 7.3 %all-to-all-start = ((s32[8,1,6]{2,1,0:T(1,128)}), s32[8,1,6]{2,1,0:T(1,128)S(1)}, u32[]{:S(2)}, u32[]{:S(2)}) async-start(s32[8,1,6]{2,1,0:T(1,128)} %bitcast.5), calls=%async_computation | async-start | bytes 8192 | tf_op jit(solution)/shard_map/all_to_all | solution.py:213
  18.2 10.9 %all-gather.2.cloned.1.call-done = bf16[4096,128]{1,0:T(8,128)(2,1)} async-done(((bf16[1024,128]{1,0:T(8,128)(2,1)}), bf16[4096,128]{1,0:T(8,128)(2,1)}) %all-gather.2.cloned.1.call-update) | async-done | bytes 1048592 | tf_op jit(solution)/shard_map/all_gather | solution.py:216
  29.0 1.5 copy.20
  30.5 12.0 %terms.1 = bf16[48,128,512]{2,1,0:T(8,128)(2,1)S(1)} custom-call(s32[48]{0:T(128)S(1)} %get-tuple-element.13.order_ref, s32[48]{0:T(128)S(1)} %get-tuple-element.12.row_ref, s32[48]{0:T(128)S(1)} %get-tuple-element.11.live_ref, bf16[8,128,512]{2,1,0:T(8,128)(2,1)S(1)} %bitcast.42, bf16[46,512,512]{2,1,0:T(8,128)(2,1)} %bitcast.43, ...), custom_call_target="tpu_custom_call" | custom-call | tf_op jit(solution)/shard_map/terms/pallas_call | solution.py:36
  42.5 2.6 copy-done
  45.2 5.5 %all-to-all-start.1 = ((bf16[8,6,128,512]{3,2,1,0:T(8,128)(2,1)}), bf16[8,6,128,512]{3,2,1,0:T(8,128)(2,1)}, u32[]{:S(2)}, u32[]{:S(2)}) async-start(bf16[8,6,128,512]{3,2,1,0:T(8,128)(2,1)} %bitcast.40), calls=%async_computation.1 | async-start | bytes 12582912 | tf_op jit(solution)/shard_map/all_to_all | solution.py:222
  50.7 0.0 reduce-scatter.2.cloned.1.call-start
  50.7 0.5 broadcast.180
  51.3 0.7 reduce.9
  51.9 0.1 reshape.124.label_ref
  52.0 137.3 %all-to-all-done.1 = bf16[8,6,128,512]{3,2,1,0:T(8,128)(2,1)} async-done(((bf16[8,6,128,512]{3,2,1,0:T(8,128)(2,1)}), bf16[8,6,128,512]{3,2,1,0:T(8,128)(2,1)}, u32[]{:S(2)}, u32[]{:S(2)}) %all-to-all-start.1) | async-done | bytes 6291488 | tf_op jit(solution)/shard_map/all_to_all | solution.py:222
  189.3 7.2 %combine.1 = bf16[48,128,512]{2,1,0:T(8,128)(2,1)S(1)} custom-call(s32[48]{0:T(128)S(1)} %reshape.124.label_ref, bf16[48,128,512]{2,1,0:T(8,128)(2,1)} %bitcast.10.arrived_ref), custom_call_target="tpu_custom_call" | custom-call | tf_op jit(solution)/shard_map/combine/pallas_call | solution.py:77
  196.6 141.7 %all_to_all.16 = bf16[8,6,128,512]{3,2,1,0:T(8,128)(2,1)S(1)} all-to-all(bf16[8,6,128,512]{3,2,1,0:T(8,128)(2,1)S(1)} %bitcast.39), channel_id=1, replica_groups=mesh['rows'=8,'cols'=4] {'rows'}, dimensions={0} | all-to-all | bytes 12582912 | tf_op jit(solution)/shard_map/all_to_all | solution.py:222
  338.3 18.1 %sample.1 = f32[8,512,128]{2,1,0:T(8,128)} custom-call(s32[48]{0:T(128)S(1)} %get-tuple-element.13.order_ref, s32[48]{0:T(128)S(1)} %get-tuple-element.12.row_ref, s32[48]{0:T(128)S(1)} %get-tuple-element.11.live_ref, bf16[48,128,512]{2,1,0:T(8,128)(2,1)S(1)} %bitcast.41, bf16[46,512,512]{2,1,0:T(8,128)(2,1)} %bitcast.49, bf16[46,512,512]{2,1,0:T(8,128)(2,1)} %bitcast.50, ...), custom_call_target="tpu_custom_call" | custom-call | tf_op jit(solution)/shard_map/sample/pallas_call | solution.py:130
  356.4 29.7 %reduce-scatter.2.cloned.1.call-done = f32[1024,128]{1,0:T(8,128)} async-done(((f32[4096,128]{1,0:T(8,128)}), f32[1024,128]{1,0:T(8,128)}) %reduce-scatter.2.cloned.1.call-update) | async-done | bytes 524304 | tf_op jit(solution)/shard_map/reduce_scatter | solution.py:228
  386.1 2.8 fusion.7.x_ref
  388.9 20.0 %gram_sum.1 = f32[5,128,128]{2,1,0:T(8,128)} custom-call(f32[128,128]{1,0:T(8,128)} %fusion.7.x_ref), custom_call_target="tpu_custom_call" | custom-call | tf_op jit(solution)/shard_map/gram_sum/pallas_call | solution.py:179
  408.9 0.8 slice.13
  409.7 0.1 copy.24
  409.8 0.1 copy.22
  409.9 11.7 %cholesky.16 = f32[128,128]{1,0:T(8,128)S(1)} custom-call(f32[128,128]{1,0:T(8,128)S(1)} %fusion), custom_call_target="Cholesky" | custom-call | tf_op jit(solution)/shard_map/jit(cholesky)/cholesky | solution.py:234
  421.7 0.6 compare_reduce_fusion
  422.3 0.7 fusion.3
  423.0 0.7 copy.23
  423.7 9.8 %custom-call.6 = f32[1,128,128]{1,2,0:T(8,128)S(1)} custom-call(f32[1,128,128]{2,1,0:T(8,128)S(1)} %get-tuple-element.15), custom_call_target="InvertDiagBlocksLowerTriangular" | custom-call | tf_op jit(solution)/shard_map/triangular_solve | solution.py:235
  433.5 2.4 fusion.1
  (9 shorter events, 0.1 us)
Async XLA Ops:
  7.2 21.9 %all-gather.2.cloned.1.call-start = ((), (), s32[]{:S(2)}) async-start(), calls=%async_computation.4 | async-start | bytes 1310720 | tf_op jit(solution)/shard_map/all_gather | solution.py:216
  10.9 34.3 %all-to-all-start = ((s32[8,1,6]{2,1,0:T(1,128)}), s32[8,1,6]{2,1,0:T(1,128)S(1)}, u32[]{:S(2)}, u32[]{:S(2)}) async-start(s32[8,1,6]{2,1,0:T(1,128)} %bitcast.5), calls=%async_computation | async-start | bytes 8192 | tf_op jit(solution)/shard_map/all_to_all | solution.py:213
  42.5 2.7 copy-start
  45.2 144.2 %all-to-all-start.1 = ((bf16[8,6,128,512]{3,2,1,0:T(8,128)(2,1)}), bf16[8,6,128,512]{3,2,1,0:T(8,128)(2,1)}, u32[]{:S(2)}, u32[]{:S(2)}) async-start(bf16[8,6,128,512]{3,2,1,0:T(8,128)(2,1)} %bitcast.40), calls=%async_computation.1 | async-start | bytes 12582912 | tf_op jit(solution)/shard_map/all_to_all | solution.py:222
  50.7 335.4 %reduce-scatter.2.cloned.1.call-start = ((), (), s32[]{:S(2)}) async-start(), calls=%async_computation.5 | async-start | bytes 2621440 | tf_op jit(solution)/shard_map/reduce_scatter | solution.py:228
Sparse Core Ops, SparseCore 0:
  9.6 19.4 all-gather.1
  356.5 29.5 reduce-scatter.1

commit v2 on v0

v2 whole, which is shorter than its diff:
```python
import functools

import jax
import jax.numpy as jnp
from jax import lax
from jax.experimental import pallas as pl
from jax.experimental.pallas import tpu as pltpu
from jax.sharding import PartitionSpec as P

RB = 8
CB_DEV = 12
MESH = pl.DeviceIdType.MESH
MIB = 1024 * 1024


def power_kernel(
    n, per, order_ref, row_ref, live_ref, before_ref, final_ref, row_before_ref, row_final_ref,
    docs_ref, tiles_ref, out_ref, tiles, send, first, second, acc,
    tile_sem, send_first, recv_first, send_second, recv_second,
):
    places = n * per
    me = lax.axis_index("rows")
    mate = lax.axis_index("cols")
    slots = tiles.shape[0]
    piece = (slots + 3) // 4
    loads = []
    for i in range(4):
        part = pl.ds(i * piece, min(piece, slots - i * piece))
        loads.append(pltpu.make_async_copy(tiles_ref.at[part], tiles.at[part], tile_sem.at[i]))
        loads[-1].start()

    barrier = pltpu.get_barrier_semaphore()
    for k in range(1, n):
        pl.semaphore_signal(
            barrier, inc=1, device_id=(lax.rem(me + k, n), mate), device_id_type=MESH
        )
    pl.semaphore_wait(barrier, n - 1)

    def offset(j):
        return (j % 2) * ((j + 1) // 2) + (1 - j % 2) * (n - j // 2)

    def out_copy(j):
        return pltpu.make_async_remote_copy(
            src_ref=send.at[j], dst_ref=first.at[j], send_sem=send_first.at[j],
            recv_sem=recv_first.at[j], device_id=((me + offset(j)) % n, mate),
            device_id_type=MESH,
        )

    def back_copy(j):
        return pltpu.make_async_remote_copy(
            src_ref=send.at[j], dst_ref=second.at[j], send_sem=send_second.at[j],
            recv_sem=recv_second.at[j], device_id=((me + n - offset(j)) % n, mate),
            device_id_type=MESH,
        )

    acc[places] = jnp.zeros(acc.shape[1:], acc.dtype)
    for load in loads:
        load.wait()

    def term(at):
        value = jnp.dot(
            docs_ref[row_ref[at]], tiles[order_ref[at]], preferred_element_type=jnp.float32
        )
        return jnp.where(live_ref[at] > 0, value, 0.0).astype(jnp.bfloat16)

    def emit_terms(t, carry):
        j = n - 1 - t
        for c in range(per):
            send[j, c] = term(j * per + c)
        out_copy(j).start()
        return carry

    lax.fori_loop(0, n - 1, emit_terms, 0)
    for c in range(per):
        first[0, c] = term(c)

    def add_arrived(j):
        for c in range(per):
            at = j * per + c
            acc[at] = first[j, c].astype(jnp.float32) + acc[before_ref[at]]

    add_arrived(0)

    def take_terms(j, carry):
        out_copy(j).wait_recv()
        add_arrived(j)
        return carry

    lax.fori_loop(1, n, take_terms, 0)

    def give_back(t, carry):
        j = n - 1 - t
        out_copy(j).wait_send()
        for c in range(per):
            send[j, c] = acc[final_ref[j * per + c]].astype(jnp.bfloat16)
        back_copy(j).start()
        return carry

    lax.fori_loop(0, n - 1, give_back, 0)
    for c in range(per):
        second[0, c] = acc[final_ref[c]].astype(jnp.bfloat16)

    def multiply(j):
        for c in range(per):
            at = j * per + c
            acc[at] = acc[row_before_ref[at]] + lax.dot_general(
                second[j, c], tiles[order_ref[at]], (((1,), (1,)), ((), ())),
                preferred_element_type=jnp.float32,
            )

    multiply(0)

    def take_loadings(j, carry):
        back_copy(j).wait_recv()
        multiply(j)
        return carry

    lax.fori_loop(1, n, take_loadings, 0)
    for r in range(RB):
        out_ref[r] = acc[row_final_ref[r]].T

    def finish(j, carry):
        back_copy(j).wait_send()
        return carry

    lax.fori_loop(1, n, finish, 0)


def power_call(order, row, live, before, final, row_before, row_final, docs, tiles, n, per):
    slots, width, _ = tiles.shape
    vectors = docs.shape[1]
    smem = pl.BlockSpec(memory_space=pltpu.SMEM)
    vmem = pl.BlockSpec(memory_space=pltpu.VMEM)
    blocks = (n, per, vectors, width)
    sems = pltpu.SemaphoreType.DMA((n,))
    return pl.pallas_call(
        functools.partial(power_kernel, n, per),
        out_shape=jax.ShapeDtypeStruct((RB, width, vectors), jnp.float32),
        in_specs=[smem] * 7 + [vmem, pl.BlockSpec(memory_space=pl.ANY)],
        out_specs=vmem,
        scratch_shapes=[
            pltpu.VMEM((slots, width, width), jnp.bfloat16),
            pltpu.VMEM(blocks, jnp.bfloat16),
            pltpu.VMEM(blocks, jnp.bfloat16),
            pltpu.VMEM(blocks, jnp.bfloat16),
            pltpu.VMEM((n * per + 1, vectors, width), jnp.float32),
            pltpu.SemaphoreType.DMA((4,)),
            sems, sems, sems, sems,
        ],
        compiler_params=pltpu.CompilerParams(
            collective_id=0, has_side_effects=True, vmem_limit_bytes=61 * MIB
        ),
        name="power_step",
    )(order, row, live, before, final, row_before, row_final, docs, tiles)


def chain(key, valid, none):
    at = jnp.arange(key.shape[0], dtype=jnp.int32)
    same = (key[:, None] == key[None, :]) & (valid[None, :] > 0)
    before = jnp.max(jnp.where(same & (at[None, :] < at[:, None]), at[None, :], -1), axis=1)
    final = jnp.max(jnp.where(same, at[None, :], -1), axis=1)
    return jnp.where(before < 0, none, before), jnp.where(final < 0, none, final)


def sum_kernel(axes, x_ref, out_ref, arrived, send_sem, recv_sem):
    place = {name: lax.axis_index(name) for name, _ in axes}
    partners = []
    for name, size in axes:
        bit = 1
        while bit < size:
            other = dict(place)
            mine = place[name]
            other[name] = jnp.where((mine // bit) % 2 == 0, mine + bit, mine - bit)
            partners.append((other["rows"], other["cols"]))
            bit *= 2
    barrier = pltpu.get_barrier_semaphore()
    for partner in partners:
        pl.semaphore_signal(barrier, inc=1, device_id=partner, device_id_type=MESH)
    pl.semaphore_wait(barrier, len(partners))
    for step, partner in enumerate(partners):
        source = x_ref if step == 0 else out_ref.at[step - 1]
        copy = pltpu.make_async_remote_copy(
            src_ref=source,
            dst_ref=arrived.at[step],
            send_sem=send_sem.at[step],
            recv_sem=recv_sem.at[step],
            device_id=partner,
            device_id_type=MESH,
        )
        copy.start()
        copy.wait()
        out_ref[step] = source[...] + arrived[step]


def sum_everywhere(x):
    axes = [("cols", lax.axis_size("cols")), ("rows", lax.axis_size("rows"))]
    steps = sum(size.bit_length() - 1 for _, size in axes)
    shape = (steps,) + x.shape
    return pl.pallas_call(
        functools.partial(sum_kernel, axes),
        out_shape=jax.ShapeDtypeStruct(shape, x.dtype),
        in_specs=[pl.BlockSpec(memory_space=pltpu.VMEM)],
        out_specs=pl.BlockSpec(memory_space=pltpu.VMEM),
        scratch_shapes=[
            pltpu.VMEM(shape, x.dtype),
            pltpu.SemaphoreType.DMA((steps,)),
            pltpu.SemaphoreType.DMA((steps,)),
        ],
        compiler_params=pltpu.CompilerParams(collective_id=1, has_side_effects=True),
        name="gram_sum",
    )(x)[steps - 1]


def local(doc_tiles, tile_rows, tile_cols, counts, start_block):
    tiles = doc_tiles[0, 0]
    rows_here = tile_rows[0, 0]
    cols_here = tile_cols[0, 0]
    slots, width, _ = tiles.shape
    vectors = start_block.shape[1]
    groups = lax.axis_size("rows")
    per_owner = (slots + groups - 1) // groups
    places = groups * per_owner
    slot_index = jnp.arange(slots, dtype=jnp.int32)
    alive = (slot_index < counts[0, 0]).astype(jnp.int32)
    owner_of = cols_here // CB_DEV
    earlier = (owner_of[:, None] == owner_of[None, :]) & (slot_index[None, :] < slot_index[:, None])
    rank = jnp.sum(earlier.astype(jnp.int32), axis=1)
    me = lax.axis_index("rows")
    away = (owner_of - me) % groups
    stop = jnp.where(2 * away <= groups, 2 * away - 1, 2 * (groups - away))
    stop = jnp.where(away == 0, 0, stop)
    target = stop * per_owner + rank
    place = jnp.arange(places, dtype=jnp.int32)
    chosen = (place[:, None] == target[None, :]).astype(jnp.int32)
    order = jnp.sum(chosen * slot_index[None, :], axis=1)
    row = jnp.sum(chosen * rows_here[None, :], axis=1)
    live = jnp.sum(chosen * alive[None, :], axis=1)
    by_owner = (place[:, None] == (owner_of * per_owner + rank)[None, :]).astype(jnp.int32)
    label = jnp.sum(by_owner * (alive * (cols_here % CB_DEV + 1))[None, :], axis=1) - 1
    labels = lax.all_to_all(
        label.reshape(groups, per_owner), "rows", split_axis=0, concat_axis=0, tiled=True
    )
    stops = jnp.arange(groups, dtype=jnp.int32)
    away_at = jnp.where(stops % 2 == 1, (stops + 1) // 2, groups - stops // 2)
    source = (me - away_at) % groups
    pick = (source[:, None] == stops[None, :]).astype(jnp.int32)
    labels = jnp.sum(pick[:, :, None] * labels[None, :, :], axis=1).reshape(places)
    before, final = chain(labels, labels >= 0, places)
    row_before, _ = chain(row, live, places)
    row_match = (jnp.arange(RB, dtype=jnp.int32)[:, None] == row[None, :]) & (live[None, :] > 0)
    row_final = jnp.max(jnp.where(row_match, place[None, :], -1), axis=1)
    row_final = jnp.where(row_final < 0, places, row_final)
    group_docs = lax.all_gather(start_block, "cols", axis=0, tiled=True)
    docs = jnp.swapaxes(group_docs.reshape(RB, width, vectors), 1, 2)
    partial_rows = power_call(
        order, row, live, before, final, row_before, row_final, docs, tiles, groups, per_owner
    )
    partial_rows = partial_rows.reshape(RB * width, vectors)
    own_rows = lax.psum_scatter(partial_rows, "cols", scatter_dimension=0, tiled=True)
    total_docs = own_rows.shape[0] * lax.axis_size("rows") * lax.axis_size("cols")
    local_gram = jnp.dot(
        own_rows.T, own_rows, precision=lax.Precision.HIGHEST, preferred_element_type=jnp.float32
    )
    gram_total = sum_everywhere(local_gram) / total_docs
    lower_factor = jnp.linalg.cholesky(gram_total)
    basis = lax.linalg.triangular_solve(
        lower_factor, own_rows, left_side=False, lower=True, transpose_a=True
    )
    return (basis, lower_factor.T)


def solution(mesh):
    placed = (
        P("rows", "cols", None, None, None),
        P("rows", "cols", None),
        P("rows", "cols", None),
        P("rows", "cols"),
        P(("rows", "cols"), None),
    )
    return jax.shard_map(
        local,
        mesh=mesh,
        in_specs=placed,
        out_specs=(P(("rows", "cols"), None), P()),
        check_vma=False,
    )
```

time: 634 us -> 446 us (0.70)
  Pallas kernels: 0 us -> 301 us
  waiting for transfers between devices: 336 us -> 84 us
  blocking collectives: 144 us -> 0 us
  matrix products: 56.3 us -> 5.23 us
  local copies, waits for them, and re-layouts: 46.2 us -> 4.96 us
    pallas_call x0 -> x2, Pallas kernels: none -> 301 us  [the longest x1 281 us: power_call(): pl.pallas_call(functools.partial(power_kernel, n, per), out_shape=jax.Sha...]
    all_gather x1 -> x0, waiting for transfers between devices: 174 us -> none  [local(): every_block = lax.all_gather(owned, 'rows', axis=0, tiled=True)]
    all_to_all x1 -> x0, blocking collectives: 144 us -> none  [local(): lax.all_to_all(outgoing, 'rows', split_axis=0, concat_axis=0, tiled=True)]
    psum x1 -> x0, waiting for transfers between devices: 122 us -> none  [local(): gram_total = lax.psum(local_gram, ('rows', 'cols')) / total_docs]
    dot_general x6 -> x0, matrix products: 51.1 us -> none  [the longest x1 17.6 us: local(): jnp.einsum('sqp,spk->sqk', tiles_here, wanted, preferred_element_type=jnp...]
    reduce_scatter x1, waiting for transfers between devices: 29.4 us -> 75.8 us  [local(): lax.psum_scatter(partial_rows, 'cols', scatter_dimension=0, tiled=True)]
    gather x2 -> x0, local copies, waits for them, and re-layouts: 15.5 us -> none  [the longest x1 9.41 us: local(): wanted = jnp.take(every_block, cols_here, axis=0)]
    convert_element_type x4 -> x0, local copies, waits for them, and re-layouts: 14.9 us -> none  [the longest x1 8.96 us: local(): tile_terms = (tile_terms * alive[:, None, None]).astype(jnp.bfloat16)]
  transfers between devices with their start and end apart: 5 -> 3, of which waited for: 4 -> 3; matrix products, arithmetic and copies ran while one was open for 7% -> 1% of each run, Pallas kernels for 0% -> 0%
where the time goes in v2:
time: 446 us; the launch traced here: 445 us
  Pallas kernels  301 us (67%)
  waiting for transfers between devices  84 us (19%)
  other arithmetic  27.5 us (6%)
  between operations  14.8 us (3%)
  starting transfers between devices  7.33 us (2%)
  matrix products  5.23 us (1%)
  local copies, waits for them, and re-layouts  4.96 us (1%)
    pallas_call x1, Pallas kernels, power_call(): pl.pallas_call(functools.partial(power_kernel, n, per), out_shape=jax.Sha...  281 us
    reduce_scatter x1, waiting for transfers between devices, local(): lax.psum_scatter(partial_rows, 'cols', scatter_dimension=0, tiled=True)  75.8 us
    pallas_call x1, Pallas kernels, sum_everywhere(): pl.pallas_call(functools.partial(sum_kernel, axes), out_shape=jax.ShapeDt...  20 us
    another operation x3, other arithmetic, local(): lower_factor = jnp.linalg.cholesky(gram_total)  12.4 us
    another operation x1, other arithmetic, local(): lax.linalg.triangular_solve(lower_factor, own_rows, left_side=False, lowe...  9.81 us
  transfers between devices with their start and end apart: 3, of which 3 were waited for; matrix products, arithmetic and copies ran while one was open for 1% of the time, Pallas kernels for 0%

profile of v2, /device:TPU:0, one launch (start us, length us, event | category | flops | bytes accessed | tf_op | source)
XLA Modules:
  0.0 445.1 jit_solution(13581773669736004608)
XLA Ops:
  7.2 0.7 all-gather.2.cloned.1.call-update
  8.5 0.7 compare_select_fusion.14
  9.2 0.2 convert_reduce_fusion
  9.4 0.1 select_reduce_fusion.4
  9.5 0.7 sub.67
  10.2 7.3 %all-to-all-start = ((s32[8,1,6]{2,1,0:T(1,128)}), s32[8,1,6]{2,1,0:T(1,128)S(1)}, u32[]{:S(2)}, u32[]{:S(2)}) async-start(s32[8,1,6]{2,1,0:T(1,128)} %bitcast.5), calls=%async_computation | async-start | bytes 8192 | tf_op jit(solution)/shard_map/all_to_all | solution.py:240
  17.5 1.3 select_reduce_fusion.5
  18.8 0.1 select_reduce_fusion.8
  19.0 0.2 select_reduce_fusion.1
  19.2 0.5 compare_select_fusion.1.row_before_ref
  19.8 0.5 compare_select_fusion.row_final_ref
  20.2 3.6 all-to-all-done
  23.9 0.2 multiply_reduce_fusion
  24.1 0.1 copy.21
  24.2 0.1 eq.132
  24.3 0.2 select_reduce_fusion.2
  24.5 0.6 compare_select_fusion.2
  25.1 3.9 all-gather.2.cloned.1.call-done
  29.0 2.3 copy.22
  31.3 281.3 %power_step.1 = f32[8,512,128]{2,1,0:T(8,128)} custom-call(s32[48]{0:T(128)} %get-tuple-element.14.order_ref, s32[48]{0:T(128)} %copy-done, s32[48]{0:T(128)} %copy-done.1, s32[48]{0:T(128)} %get-tuple-element.22.before_ref, s32[48]{0:T(128)} %get-tuple-element.21.final_ref, s32[48]{0:T(128)} %compare_select_fusion.1.row_before_ref, ...), custom_call_target="tpu_custom_call" | custom-call | tf_op jit(solution)/shard_map/power_step/pallas_call | solution.py:136
  312.6 75.8 %reduce-scatter.2.cloned.1.call-done = f32[1024,128]{1,0:T(8,128)} async-done(((f32[4096,128]{1,0:T(8,128)}), f32[1024,128]{1,0:T(8,128)}) %reduce-scatter.2.cloned.1.call-update) | async-done | bytes 524304 | tf_op jit(solution)/shard_map/reduce_scatter | solution.py:259
  388.4 2.8 fusion.19.x_ref
  391.2 20.0 %gram_sum.1 = f32[5,128,128]{2,1,0:T(8,128)} custom-call(f32[128,128]{1,0:T(8,128)} %fusion.19.x_ref), custom_call_target="tpu_custom_call" | custom-call | tf_op jit(solution)/shard_map/gram_sum/pallas_call | solution.py:199
  411.2 0.8 slice.13
  412.1 0.1 copy.26
  412.2 0.1 copy.24
  412.3 11.7 %cholesky.16 = f32[128,128]{1,0:T(8,128)S(1)} custom-call(f32[128,128]{1,0:T(8,128)S(1)} %fusion), custom_call_target="Cholesky" | custom-call | tf_op jit(solution)/shard_map/jit(cholesky)/cholesky | solution.py:265
  424.0 0.6 compare_reduce_fusion
  424.7 0.7 fusion.3
  425.4 0.7 copy.25
  426.1 9.8 %custom-call.6 = f32[1,128,128]{1,2,0:T(8,128)S(1)} custom-call(f32[1,128,128]{2,1,0:T(8,128)S(1)} %get-tuple-element.16), custom_call_target="InvertDiagBlocksLowerTriangular" | custom-call | tf_op jit(solution)/shard_map/triangular_solve | solution.py:266
  435.9 2.4 fusion.1
  (18 shorter events, 0.4 us)
Async XLA Ops:
  7.2 21.9 %all-gather.2.cloned.1.call-start = ((), (), s32[]{:S(2)}) async-start(), calls=%async_computation.2 | async-start | bytes 1310720 | tf_op jit(solution)/shard_map/all_gather | solution.py:253
  10.2 13.6 %all-to-all-start = ((s32[8,1,6]{2,1,0:T(1,128)}), s32[8,1,6]{2,1,0:T(1,128)S(1)}, u32[]{:S(2)}, u32[]{:S(2)}) async-start(s32[8,1,6]{2,1,0:T(1,128)} %bitcast.5), calls=%async_computation | async-start | bytes 8192 | tf_op jit(solution)/shard_map/all_to_all | solution.py:240
  17.5 370.9 %reduce-scatter.2.cloned.1.call-start = ((), (), s32[]{:S(2)}) async-start(), calls=%async_computation.3 | async-start | bytes 2621440 | tf_op jit(solution)/shard_map/reduce_scatter | solution.py:259
  18.8 12.5 %copy-start = (s32[48]{0:T(128)}, s32[48]{0:T(128)S(1)}, u32[]{:S(2)}) copy-start(s32[48]{0:T(128)S(1)} %get-tuple-element.13.row_ref) | copy-start | bytes 580
  18.8 12.5 %copy-start.1 = (s32[48]{0:T(128)}, s32[48]{0:T(128)S(1)}, u32[]{:S(2)}) copy-start(s32[48]{0:T(128)S(1)} %get-tuple-element.12.live_ref) | copy-start | bytes 580
Sparse Core Ops, SparseCore 0:
  9.6 19.4 all-gather.1
  312.7 75.6 reduce-scatter.1

commit v3 on v2

--- a/solution.py
+++ b/solution.py
@@ -11,6 +11,14 @@
 CB_DEV = 12
 MESH = pl.DeviceIdType.MESH
 MIB = 1024 * 1024
+
+
+def paired(me, j, n):
+    other, bit = 0, 1
+    while bit < n:
+        other = other + bit * ((me // bit + j // bit) % 2)
+        bit *= 2
+    return other
 
 
 def power_kernel(
@@ -36,20 +44,20 @@
         )
     pl.semaphore_wait(barrier, n - 1)
 
-    def offset(j):
-        return (j % 2) * ((j + 1) // 2) + (1 - j % 2) * (n - j // 2)
+    def partner(j):
+        return paired(me, j, n)
 
     def out_copy(j):
         return pltpu.make_async_remote_copy(
             src_ref=send.at[j], dst_ref=first.at[j], send_sem=send_first.at[j],
-            recv_sem=recv_first.at[j], device_id=((me + offset(j)) % n, mate),
+            recv_sem=recv_first.at[j], device_id=(partner(j), mate),
             device_id_type=MESH,
         )
 
     def back_copy(j):
         return pltpu.make_async_remote_copy(
             src_ref=send.at[j], dst_ref=second.at[j], send_sem=send_second.at[j],
-            recv_sem=recv_second.at[j], device_id=((me + n - offset(j)) % n, mate),
+            recv_sem=recv_second.at[j], device_id=(partner(j), mate),
             device_id_type=MESH,
         )
 
@@ -162,53 +170,98 @@
     return jnp.where(before < 0, none, before), jnp.where(final < 0, none, final)
 
 
-def sum_kernel(axes, x_ref, out_ref, arrived, send_sem, recv_sem):
+def tail_kernel(
+    axes, total, part_ref, own_ref, gram_ref, work, land, grams, arrived,
+    send_sem, recv_sem, gram_send, gram_recv,
+):
     place = {name: lax.axis_index(name) for name, _ in axes}
     partners = []
     for name, size in axes:
         bit = 1
         while bit < size:
             other = dict(place)
-            mine = place[name]
-            other[name] = jnp.where((mine // bit) % 2 == 0, mine + bit, mine - bit)
+            other[name] = paired(place[name], bit, size)
             partners.append((other["rows"], other["cols"]))
             bit *= 2
     barrier = pltpu.get_barrier_semaphore()
     for partner in partners:
         pl.semaphore_signal(barrier, inc=1, device_id=partner, device_id_type=MESH)
     pl.semaphore_wait(barrier, len(partners))
+
+    me, cols = place["cols"], part_ref.shape[0]
+    bit, step, base = 1, 0, 0
+    while bit < cols:
+        source = part_ref if step == 0 else work
+        mine = (me // bit) % 2
+        count = cols // (2 * bit)
+        copies = []
+        for t in range(count):
+            given = me % bit + bit * (1 - mine) + 2 * bit * t
+            copy = pltpu.make_async_remote_copy(
+                src_ref=source.at[given],
+                dst_ref=land.at[base + t],
+                send_sem=send_sem.at[base + t],
+                recv_sem=recv_sem.at[base + t],
+                device_id=partners[step],
+                device_id_type=MESH,
+            )
+            copy.start()
+            copies.append(copy)
+        for t in range(count):
+            kept = me % bit + bit * mine + 2 * bit * t
+            copies[t].wait()
+            work[kept] = source[kept] + land[base + t]
+        base += count
+        step += 1
+        bit *= 2
+    own = work[me]
+    own_ref[...] = own
+    grams[0] = jnp.dot(
+        own.T, own, precision=lax.Precision.HIGHEST, preferred_element_type=jnp.float32
+    )
     for step, partner in enumerate(partners):
-        source = x_ref if step == 0 else out_ref.at[step - 1]
         copy = pltpu.make_async_remote_copy(
-            src_ref=source,
+            src_ref=grams.at[step],
             dst_ref=arrived.at[step],
-            send_sem=send_sem.at[step],
-            recv_sem=recv_sem.at[step],
+            send_sem=gram_send.at[step],
+            recv_sem=gram_recv.at[step],
             device_id=partner,
             device_id_type=MESH,
         )
         copy.start()
         copy.wait()
-        out_ref[step] = source[...] + arrived[step]
-
-
-def sum_everywhere(x):
-    axes = [("cols", lax.axis_size("cols")), ("rows", lax.axis_size("rows"))]
+        grams[step + 1] = grams[step] + arrived[step]
+    gram_ref[...] = grams[len(partners)] / total
+
+
+def tail_call(part, total):
+    cols, rows, vectors = part.shape
+    axes = [("cols", cols), ("rows", lax.axis_size("rows"))]
     steps = sum(size.bit_length() - 1 for _, size in axes)
-    shape = (steps,) + x.shape
+    vmem = pl.BlockSpec(memory_space=pltpu.VMEM)
     return pl.pallas_call(
-        functools.partial(sum_kernel, axes),
-        out_shape=jax.ShapeDtypeStruct(shape, x.dtype),
-        in_specs=[pl.BlockSpec(memory_space=pltpu.VMEM)],
-        out_specs=pl.BlockSpec(memory_space=pltpu.VMEM),
+        functools.partial(tail_kernel, axes, float(total)),
+        out_shape=(
+            jax.ShapeDtypeStruct((rows, vectors), jnp.float32),
+            jax.ShapeDtypeStruct((vectors, vectors), jnp.float32),
+        ),
+        in_specs=[vmem],
+        out_specs=(vmem, vmem),
         scratch_shapes=[
-            pltpu.VMEM(shape, x.dtype),
+            pltpu.VMEM(part.shape, jnp.float32),
+            pltpu.VMEM((cols - 1, rows, vectors), jnp.float32),
+            pltpu.VMEM((steps + 1, vectors, vectors), jnp.float32),
+            pltpu.VMEM((steps, vectors, vectors), jnp.float32),
+            pltpu.SemaphoreType.DMA((cols - 1,)),
+            pltpu.SemaphoreType.DMA((cols - 1,)),
             pltpu.SemaphoreType.DMA((steps,)),
             pltpu.SemaphoreType.DMA((steps,)),
         ],
-        compiler_params=pltpu.CompilerParams(collective_id=1, has_side_effects=True),
-        name="gram_sum",
-    )(x)[steps - 1]
+        compiler_params=pltpu.CompilerParams(
+            collective_id=1, has_side_effects=True, vmem_limit_bytes=24 * MIB
+        ),
+        name="sum_and_gram",
+    )(part)
 
 
 def local(doc_tiles, tile_rows, tile_cols, counts, start_block):
@@ -226,10 +279,7 @@
     earlier = (owner_of[:, None] == owner_of[None, :]) & (slot_index[None, :] < slot_index[:, None])
     rank = jnp.sum(earlier.astype(jnp.int32), axis=1)
     me = lax.axis_index("rows")
-    away = (owner_of - me) % groups
-    stop = jnp.where(2 * away <= groups, 2 * away - 1, 2 * (groups - away))
-    stop = jnp.where(away == 0, 0, stop)
-    target = stop * per_owner + rank
+    target = (owner_of ^ me) * per_owner + rank
     place = jnp.arange(places, dtype=jnp.int32)
     chosen = (place[:, None] == target[None, :]).astype(jnp.int32)
     order = jnp.sum(chosen * slot_index[None, :], axis=1)
@@ -241,9 +291,7 @@
         label.reshape(groups, per_owner), "rows", split_axis=0, concat_axis=0, tiled=True
     )
     stops = jnp.arange(groups, dtype=jnp.int32)
-    away_at = jnp.where(stops % 2 == 1, (stops + 1) // 2, groups - stops // 2)
-    source = (me - away_at) % groups
-    pick = (source[:, None] == stops[None, :]).astype(jnp.int32)
+    pick = ((stops ^ me)[:, None] == stops[None, :]).astype(jnp.int32)
     labels = jnp.sum(pick[:, :, None] * labels[None, :, :], axis=1).reshape(places)
     before, final = chain(labels, labels >= 0, places)
     row_before, _ = chain(row, live, places)
@@ -255,13 +303,11 @@
     partial_rows = power_call(
         order, row, live, before, final, row_before, row_final, docs, tiles, groups, per_owner
     )
-    partial_rows = partial_rows.reshape(RB * width, vectors)
-    own_rows = lax.psum_scatter(partial_rows, "cols", scatter_dimension=0, tiled=True)
-    total_docs = own_rows.shape[0] * lax.axis_size("rows") * lax.axis_size("cols")
-    local_gram = jnp.dot(
-        own_rows.T, own_rows, precision=lax.Precision.HIGHEST, preferred_element_type=jnp.float32
-    )
-    gram_total = sum_everywhere(local_gram) / total_docs
+    cols = lax.axis_size("cols")
+    total_docs = RB * width * groups
+    own_rows, gram_total = tail_call(
+        partial_rows.reshape(cols, RB * width // cols, vectors), total_docs
+    )
     lower_factor = jnp.linalg.cholesky(gram_total)
     basis = lax.linalg.triangular_solve(
         lower_factor, own_rows, left_side=False, lower=True, transpose_a=True

time: 446 us -> 413 us (0.926)
  waiting for transfers between devices: 84 us -> 8.29 us
  Pallas kernels: 301 us -> 348 us
    reduce_scatter x1 -> x0, waiting for transfers between devices: 75.8 us -> none  [local(): lax.psum_scatter(partial_rows, 'cols', scatter_dimension=0, tiled=True)]
    pallas_call x1, Pallas kernels: 281 us -> 315 us  [power_call(): pl.pallas_call(functools.partial(power_kernel, n, per), out_shape=jax.Sha...]
    pallas_call x1, Pallas kernels: 20 us -> 32.6 us  [tail_call(): pl.pallas_call(functools.partial(tail_kernel, axes, float(total)), out_sh...]
  transfers between devices with their start and end apart: 3 -> 2, of which waited for: 3 -> 2; matrix products, arithmetic and copies ran while one was open for 1% -> 1% of each run, Pallas kernels for 0% -> 0%
where the time goes in v3:
time: 413 us
  Pallas kernels  348 us (84%)
  other arithmetic  27.5 us (7%)
  between operations  14.8 us (4%)
  waiting for transfers between devices  8.29 us (2%)
  starting transfers between devices  7.29 us (2%)
  local copies, waits for them, and re-layouts  5.61 us (1%)
    pallas_call x1, Pallas kernels, power_call(): pl.pallas_call(functools.partial(power_kernel, n, per), out_shape=jax.Sha...  315 us
    pallas_call x1, Pallas kernels, tail_call(): pl.pallas_call(functools.partial(tail_kernel, axes, float(total)), out_sh...  32.6 us
    another operation x3, other arithmetic, local(): lower_factor = jnp.linalg.cholesky(gram_total)  12.4 us
    another operation x1, other arithmetic, local(): lax.linalg.triangular_solve(lower_factor, own_rows, left_side=False, lowe...  9.81 us
  transfers between devices with their start and end apart: 2, of which 2 were waited for; matrix products, arithmetic and copies ran while one was open for 1% of the time, Pallas kernels for 0%

profile of v3, /device:TPU:0, one launch (start us, length us, event | category | flops | bytes accessed | tf_op | source)
XLA Modules:
  0.0 412.6 jit_solution(5486079965694759357)
XLA Ops:
  7.2 0.0 all-gather.2.cloned.1.call-start
  7.2 0.7 all-gather.2.cloned.1.call-update
  8.5 0.7 compare_select_fusion.4
  9.2 0.2 convert_reduce_fusion
  9.4 0.1 select_reduce_fusion.4
  9.5 0.7 sub.14
  10.2 7.3 %all-to-all-start = ((s32[8,1,6]{2,1,0:T(1,128)}), s32[8,1,6]{2,1,0:T(1,128)S(1)}, u32[]{:S(2)}, u32[]{:S(2)}) async-start(s32[8,1,6]{2,1,0:T(1,128)} %bitcast.5), calls=%async_computation | async-start | bytes 8192 | tf_op jit(solution)/shard_map/all_to_all | solution.py:290
  17.5 1.3 select_reduce_fusion.5
  18.8 0.1 select_reduce_fusion.8
  18.9 0.2 select_reduce_fusion.1
  19.1 0.5 compare_select_fusion.1.row_before_ref
  19.6 0.1 fusion.7
  19.7 0.5 compare_select_fusion.row_final_ref
  20.2 3.7 all-to-all-done
  23.9 0.1 copy.17
  23.9 0.2 multiply_reduce_fusion
  24.1 0.1 copy.18
  24.2 0.1 eq.111
  24.3 0.2 select_reduce_fusion.2
  24.5 0.6 compare_select_fusion.2
  25.1 3.9 all-gather.2.cloned.1.call-done
  29.0 2.3 copy.19
  31.3 315.2 %power_step.1 = f32[8,512,128]{2,1,0:T(8,128)} custom-call(s32[48]{0:T(128)} %get-tuple-element.18.order_ref, s32[48]{0:T(128)} %copy-done.1, s32[48]{0:T(128)} %copy-done.2, s32[48]{0:T(128)} %get-tuple-element.26.before_ref, s32[48]{0:T(128)} %get-tuple-element.25.final_ref, s32[48]{0:T(128)} %compare_select_fusion.1.row_before_ref, ...), custom_call_target="tpu_custom_call" | custom-call | tf_op jit(solution)/shard_map/power_step/pallas_call | solution.py:144
  346.5 1.6 copy-done
  348.1 32.6 %sum_and_gram.1 = (f32[1024,128]{1,0:T(8,128)S(1)}, f32[128,128]{1,0:T(8,128)S(1)}) custom-call(f32[4,1024,128]{2,1,0:T(8,128)S(1)} %bitcast.31), custom_call_target="tpu_custom_call" | custom-call | tf_op jit(solution)/shard_map/sum_and_gram/pallas_call | solution.py:242
  380.7 0.1 copy.20
  380.8 11.7 %cholesky.16 = f32[128,128]{1,0:T(8,128)S(1)} custom-call(f32[128,128]{1,0:T(8,128)S(1)} %fusion.2), custom_call_target="Cholesky" | custom-call | tf_op jit(solution)/shard_map/jit(cholesky)/cholesky | solution.py:311
  392.5 0.6 compare_reduce_fusion
  393.2 0.7 fusion.3
  393.8 0.7 copy.21
  394.6 9.8 %custom-call.6 = f32[1,128,128]{1,2,0:T(8,128)S(1)} custom-call(f32[1,128,128]{2,1,0:T(8,128)S(1)} %get-tuple-element.20), custom_call_target="InvertDiagBlocksLowerTriangular" | custom-call | tf_op jit(solution)/shard_map/triangular_solve | solution.py:312
  404.4 1.4 fusion
  (13 shorter events, 0.1 us)
Async XLA Ops:
  7.2 21.9 %all-gather.2.cloned.1.call-start = ((), (), s32[]{:S(2)}) async-start(), calls=%async_computation.1 | async-start | bytes 1310720 | tf_op jit(solution)/shard_map/all_gather | solution.py:301
  10.2 13.6 %all-to-all-start = ((s32[8,1,6]{2,1,0:T(1,128)}), s32[8,1,6]{2,1,0:T(1,128)S(1)}, u32[]{:S(2)}, u32[]{:S(2)}) async-start(s32[8,1,6]{2,1,0:T(1,128)} %bitcast.5), calls=%async_computation | async-start | bytes 8192 | tf_op jit(solution)/shard_map/all_to_all | solution.py:290
  18.8 12.5 %copy-start.1 = (s32[48]{0:T(128)}, s32[48]{0:T(128)S(1)}, u32[]{:S(2)}) copy-start(s32[48]{0:T(128)S(1)} %get-tuple-element.17.row_ref) | copy-start | bytes 580
  18.8 12.5 %copy-start.2 = (s32[48]{0:T(128)}, s32[48]{0:T(128)S(1)}, u32[]{:S(2)}) copy-start(s32[48]{0:T(128)S(1)} %get-tuple-element.16.live_ref) | copy-start | bytes 580
  346.5 1.6 copy-start
Sparse Core Ops, SparseCore 0:
  9.6 19.4 all-gather.1

commit v4 on v3

--- a/solution.py
+++ b/solution.py
@@ -47,19 +47,21 @@
     def partner(j):
         return paired(me, j, n)
 
-    def out_copy(j):
+    def out_copy(c, j):
         return pltpu.make_async_remote_copy(
-            src_ref=send.at[j], dst_ref=first.at[j], send_sem=send_first.at[j],
-            recv_sem=recv_first.at[j], device_id=(partner(j), mate),
-            device_id_type=MESH,
-        )
-
-    def back_copy(j):
+            src_ref=send.at[c, j], dst_ref=first.at[c, j], send_sem=send_first.at[c, j],
+            recv_sem=recv_first.at[c, j], device_id=(partner(j), mate), device_id_type=MESH,
+        )
+
+    def back_copy(c, j):
         return pltpu.make_async_remote_copy(
-            src_ref=send.at[j], dst_ref=second.at[j], send_sem=send_second.at[j],
-            recv_sem=recv_second.at[j], device_id=(partner(j), mate),
-            device_id_type=MESH,
-        )
+            src_ref=send.at[c, j], dst_ref=second.at[c, j], send_sem=send_second.at[c, j],
+            recv_sem=recv_second.at[c, j], device_id=(partner(j), mate), device_id_type=MESH,
+        )
+
+    turns = [n // 2]
+    for near in range(1, n // 2):
+        turns += [near, n // 2 + near]
 
     acc[places] = jnp.zeros(acc.shape[1:], acc.dtype)
     for load in loads:
@@ -71,67 +73,56 @@
         )
         return jnp.where(live_ref[at] > 0, value, 0.0).astype(jnp.bfloat16)
 
-    def emit_terms(t, carry):
-        j = n - 1 - t
-        for c in range(per):
-            send[j, c] = term(j * per + c)
-        out_copy(j).start()
-        return carry
-
-    lax.fori_loop(0, n - 1, emit_terms, 0)
-    for c in range(per):
-        first[0, c] = term(c)
-
-    def add_arrived(j):
-        for c in range(per):
-            at = j * per + c
-            acc[at] = first[j, c].astype(jnp.float32) + acc[before_ref[at]]
-
-    add_arrived(0)
-
-    def take_terms(j, carry):
-        out_copy(j).wait_recv()
-        add_arrived(j)
-        return carry
-
-    lax.fori_loop(1, n, take_terms, 0)
-
-    def give_back(t, carry):
-        j = n - 1 - t
-        out_copy(j).wait_send()
-        for c in range(per):
-            send[j, c] = acc[final_ref[j * per + c]].astype(jnp.bfloat16)
-        back_copy(j).start()
-        return carry
-
-    lax.fori_loop(0, n - 1, give_back, 0)
-    for c in range(per):
-        second[0, c] = acc[final_ref[c]].astype(jnp.bfloat16)
-
-    def multiply(j):
-        for c in range(per):
-            at = j * per + c
+    def emit_terms(c, carry):
+        for j in turns:
+            send[c, j] = term(c * n + j)
+            out_copy(c, j).start()
+        return carry
+
+    def own_terms(c, carry):
+        first[c, 0] = term(c * n)
+        return carry
+
+    def take_terms(c, carry):
+        for j in range(n):
+            if j > 0:
+                out_copy(c, j).wait_recv()
+            at = c * n + j
+            acc[at] = first[c, j].astype(jnp.float32) + acc[before_ref[at]]
+        return carry
+
+    def give_back(c, carry):
+        for j in turns:
+            out_copy(c, j).wait_send()
+            send[c, j] = acc[final_ref[c * n + j]].astype(jnp.bfloat16)
+            back_copy(c, j).start()
+        return carry
+
+    def own_loadings(c, carry):
+        second[c, 0] = acc[final_ref[c * n]].astype(jnp.bfloat16)
+        return carry
+
+    def take_loadings(c, carry):
+        for j in range(n):
+            if j > 0:
+                back_copy(c, j).wait_recv()
+            at = c * n + j
             acc[at] = acc[row_before_ref[at]] + lax.dot_general(
-                second[j, c], tiles[order_ref[at]], (((1,), (1,)), ((), ())),
+                second[c, j], tiles[order_ref[at]], (((1,), (1,)), ((), ())),
                 preferred_element_type=jnp.float32,
             )
-
-    multiply(0)
-
-    def take_loadings(j, carry):
-        back_copy(j).wait_recv()
-        multiply(j)
-        return carry
-
-    lax.fori_loop(1, n, take_loadings, 0)
+        return carry
+
+    def finish(c, carry):
+        for j in turns:
+            back_copy(c, j).wait_send()
+        return carry
+
+    for stage in (emit_terms, own_terms, take_terms, give_back, own_loadings, take_loadings):
+        lax.fori_loop(0, per, stage, 0)
     for r in range(RB):
         out_ref[r] = acc[row_final_ref[r]].T
-
-    def finish(j, carry):
-        back_copy(j).wait_send()
-        return carry
-
-    lax.fori_loop(1, n, finish, 0)
+    lax.fori_loop(0, per, finish, 0)
 
 
 def power_call(order, row, live, before, final, row_before, row_final, docs, tiles, n, per):
@@ -139,8 +130,8 @@
     vectors = docs.shape[1]
     smem = pl.BlockSpec(memory_space=pltpu.SMEM)
     vmem = pl.BlockSpec(memory_space=pltpu.VMEM)
-    blocks = (n, per, vectors, width)
-    sems = pltpu.SemaphoreType.DMA((n,))
+    blocks = (per, n, vectors, width)
+    sems = pltpu.SemaphoreType.DMA((per, n))
     return pl.pallas_call(
         functools.partial(power_kernel, n, per),
         out_shape=jax.ShapeDtypeStruct((RB, width, vectors), jnp.float32),
@@ -279,7 +270,7 @@
     earlier = (owner_of[:, None] == owner_of[None, :]) & (slot_index[None, :] < slot_index[:, None])
     rank = jnp.sum(earlier.astype(jnp.int32), axis=1)
     me = lax.axis_index("rows")
-    target = (owner_of ^ me) * per_owner + rank
+    target = rank * groups + (owner_of ^ me)
     place = jnp.arange(places, dtype=jnp.int32)
     chosen = (place[:, None] == target[None, :]).astype(jnp.int32)
     order = jnp.sum(chosen * slot_index[None, :], axis=1)
@@ -292,7 +283,7 @@
     )
     stops = jnp.arange(groups, dtype=jnp.int32)
     pick = ((stops ^ me)[:, None] == stops[None, :]).astype(jnp.int32)
-    labels = jnp.sum(pick[:, :, None] * labels[None, :, :], axis=1).reshape(places)
+    labels = jnp.sum(pick[:, :, None] * labels[None, :, :], axis=1).T.reshape(places)
     before, final = chain(labels, labels >= 0, places)
     row_before, _ = chain(row, live, places)
     row_match = (jnp.arange(RB, dtype=jnp.int32)[:, None] == row[None, :]) & (live[None, :] > 0)

time: 413 us -> 387 us (0.937)
  Pallas kernels: 348 us -> 322 us
    pallas_call x1, Pallas kernels: 315 us -> 283 us  [power_call(): pl.pallas_call(functools.partial(power_kernel, n, per), out_shape=jax.Sha...]
    pallas_call x1, Pallas kernels: 32.6 us -> 38.7 us  [tail_call(): pl.pallas_call(functools.partial(tail_kernel, axes, float(total)), out_sh...]
where the time goes in v4:
time: 387 us; the launch traced here: 386 us
  Pallas kernels  322 us (83%)
  other arithmetic  27.5 us (7%)
  between operations  14.8 us (4%)
  waiting for transfers between devices  8.37 us (2%)
  starting transfers between devices  7.29 us (2%)
  local copies, waits for them, and re-layouts  5.53 us (1%)
    pallas_call x1, Pallas kernels, power_call(): pl.pallas_call(functools.partial(power_kernel, n, per), out_shape=jax.Sha...  283 us
    pallas_call x1, Pallas kernels, tail_call(): pl.pallas_call(functools.partial(tail_kernel, axes, float(total)), out_sh...  38.7 us
    another operation x3, other arithmetic, local(): lower_factor = jnp.linalg.cholesky(gram_total)  12.4 us
    another operation x1, other arithmetic, local(): lax.linalg.triangular_solve(lower_factor, own_rows, left_side=False, lowe...  9.81 us
  transfers between devices with their start and end apart: 2, of which 2 were waited for; matrix products, arithmetic and copies ran while one was open for 1% of the time, Pallas kernels for 0%

profile of v4, /device:TPU:0, one launch (start us, length us, event | category | flops | bytes accessed | tf_op | source)
XLA Modules:
  0.0 386.5 jit_solution(14855713127255526331)
XLA Ops:
  7.2 0.0 all-gather.2.cloned.1.call-start
  7.2 0.7 all-gather.2.cloned.1.call-update
  8.5 0.7 compare_select_fusion.4
  9.2 0.2 convert_reduce_fusion
  9.4 0.1 select_reduce_fusion.4
  9.5 0.7 sub.14
  10.2 7.3 %all-to-all-start = ((s32[8,1,6]{2,1,0:T(1,128)}), s32[8,1,6]{2,1,0:T(1,128)S(1)}, u32[]{:S(2)}, u32[]{:S(2)}) async-start(s32[8,1,6]{2,1,0:T(1,128)} %bitcast.5), calls=%async_computation | async-start | bytes 8192 | tf_op jit(solution)/shard_map/all_to_all | solution.py:281
  17.5 1.3 select_reduce_fusion.5
  18.8 0.1 select_reduce_fusion.8
  18.9 0.2 select_reduce_fusion.1
  19.1 0.5 compare_select_fusion.1.row_before_ref
  19.6 0.1 fusion.7
  19.7 0.5 compare_select_fusion.row_final_ref
  20.2 3.7 all-to-all-done
  23.9 0.1 copy.17
  23.9 0.2 multiply_reduce_fusion
  24.1 0.1 eq.111
  24.2 0.2 select_reduce_fusion.2
  24.4 0.6 compare_select_fusion.2
  25.0 4.0 %all-gather.2.cloned.1.call-done = bf16[4096,128]{1,0:T(8,128)(2,1)} async-done(((bf16[1024,128]{1,0:T(8,128)(2,1)}), bf16[4096,128]{1,0:T(8,128)(2,1)}) %all-gather.2.cloned.1.call-update) | async-done | bytes 1048592 | tf_op jit(solution)/shard_map/all_gather | solution.py:292
  29.0 2.3 copy.18
  31.3 0.0 copy-done.1
  31.3 283.0 %power_step.1 = f32[8,512,128]{2,1,0:T(8,128)} custom-call(s32[48]{0:T(128)} %get-tuple-element.18.order_ref, s32[48]{0:T(128)} %copy-done.1, s32[48]{0:T(128)} %copy-done.2, s32[48]{0:T(128)} %get-tuple-element.26.before_ref, s32[48]{0:T(128)} %get-tuple-element.25.final_ref, s32[48]{0:T(128)} %compare_select_fusion.1.row_before_ref, ...), custom_call_target="tpu_custom_call" | custom-call | tf_op jit(solution)/shard_map/power_step/pallas_call | solution.py:135
  314.3 1.6 copy-done
  315.9 38.7 %sum_and_gram.1 = (f32[1024,128]{1,0:T(8,128)S(1)}, f32[128,128]{1,0:T(8,128)S(1)}) custom-call(f32[4,1024,128]{2,1,0:T(8,128)S(1)} %bitcast.32), custom_call_target="tpu_custom_call" | custom-call | tf_op jit(solution)/shard_map/sum_and_gram/pallas_call | solution.py:233
  354.6 0.1 copy.19
  354.7 11.7 %cholesky.16 = f32[128,128]{1,0:T(8,128)S(1)} custom-call(f32[128,128]{1,0:T(8,128)S(1)} %fusion.2), custom_call_target="Cholesky" | custom-call | tf_op jit(solution)/shard_map/jit(cholesky)/cholesky | solution.py:302
  366.4 0.6 compare_reduce_fusion
  367.1 0.7 fusion.3
  367.7 0.7 copy.20
  368.5 9.8 %custom-call.6 = f32[1,128,128]{1,2,0:T(8,128)S(1)} custom-call(f32[1,128,128]{2,1,0:T(8,128)S(1)} %get-tuple-element.20), custom_call_target="InvertDiagBlocksLowerTriangular" | custom-call | tf_op jit(solution)/shard_map/triangular_solve | solution.py:303
  378.3 1.4 fusion
  (12 shorter events, 0.1 us)
Async XLA Ops:
  7.2 21.9 %all-gather.2.cloned.1.call-start = ((), (), s32[]{:S(2)}) async-start(), calls=%async_computation.1 | async-start | bytes 1310720 | tf_op jit(solution)/shard_map/all_gather | solution.py:292
  10.2 13.6 %all-to-all-start = ((s32[8,1,6]{2,1,0:T(1,128)}), s32[8,1,6]{2,1,0:T(1,128)S(1)}, u32[]{:S(2)}, u32[]{:S(2)}) async-start(s32[8,1,6]{2,1,0:T(1,128)} %bitcast.5), calls=%async_computation | async-start | bytes 8192 | tf_op jit(solution)/shard_map/all_to_all | solution.py:281
  18.8 12.5 %copy-start.1 = (s32[48]{0:T(128)}, s32[48]{0:T(128)S(1)}, u32[]{:S(2)}) copy-start(s32[48]{0:T(128)S(1)} %get-tuple-element.17.row_ref) | copy-start | bytes 580
  18.8 12.5 %copy-start.2 = (s32[48]{0:T(128)}, s32[48]{0:T(128)S(1)}, u32[]{:S(2)}) copy-start(s32[48]{0:T(128)S(1)} %get-tuple-element.16.live_ref) | copy-start | bytes 580
  314.3 1.6 copy-start
Sparse Core Ops, SparseCore 0:
  9.6 19.4 all-gather.1

commit v5 on v4

--- a/solution.py
+++ b/solution.py
@@ -59,9 +59,11 @@
             recv_sem=recv_second.at[c, j], device_id=(partner(j), mate), device_id_type=MESH,
         )
 
-    turns = [n // 2]
-    for near in range(1, n // 2):
-        turns += [near, n // 2 + near]
+    def turn(i):
+        i = (i + (mate % 2) * (n // 2 + 1)) % (n - 1)
+        return (i % 2) * ((i + 1) // 2) + (1 - i % 2) * (n // 2 + i // 2)
+
+    turns = [turn(i) for i in range(n - 1)]
 
     acc[places] = jnp.zeros(acc.shape[1:], acc.dtype)
     for load in loads:

time: 387 us -> 387 us (level)
  no operation moved by 1% of the time
where the time goes in v5:
time: 387 us
  Pallas kernels  322 us (83%)
  other arithmetic  27.5 us (7%)
  between operations  14.8 us (4%)
  waiting for transfers between devices  8.37 us (2%)
  starting transfers between devices  7.29 us (2%)
  local copies, waits for them, and re-layouts  5.53 us (1%)
    pallas_call x1, Pallas kernels, power_call(): pl.pallas_call(functools.partial(power_kernel, n, per), out_shape=jax.Sha...  283 us
    pallas_call x1, Pallas kernels, tail_call(): pl.pallas_call(functools.partial(tail_kernel, axes, float(total)), out_sh...  38.6 us
    another operation x3, other arithmetic, local(): lower_factor = jnp.linalg.cholesky(gram_total)  12.4 us
    another operation x1, other arithmetic, local(): lax.linalg.triangular_solve(lower_factor, own_rows, left_side=False, lowe...  9.81 us
  transfers between devices with their start and end apart: 2, of which 2 were waited for; matrix products, arithmetic and copies ran while one was open for 1% of the time, Pallas kernels for 0%

profile of v5, /device:TPU:0, one launch (start us, length us, event | category | flops | bytes accessed | tf_op | source)
XLA Modules:
  0.0 386.6 jit_solution(6576292527828806664)
XLA Ops:
  7.2 0.0 all-gather.2.cloned.1.call-start
  7.2 0.7 all-gather.2.cloned.1.call-update
  8.5 0.7 compare_select_fusion.4
  9.2 0.2 convert_reduce_fusion
  9.4 0.1 select_reduce_fusion.4
  9.5 0.7 sub.14
  10.2 7.3 %all-to-all-start = ((s32[8,1,6]{2,1,0:T(1,128)}), s32[8,1,6]{2,1,0:T(1,128)S(1)}, u32[]{:S(2)}, u32[]{:S(2)}) async-start(s32[8,1,6]{2,1,0:T(1,128)} %bitcast.5), calls=%async_computation | async-start | bytes 8192 | tf_op jit(solution)/shard_map/all_to_all | solution.py:283
  17.5 1.3 select_reduce_fusion.5
  18.8 0.1 select_reduce_fusion.8
  18.9 0.2 select_reduce_fusion.1
  19.1 0.5 compare_select_fusion.1.row_before_ref
  19.6 0.1 fusion.7
  19.7 0.5 compare_select_fusion.row_final_ref
  20.2 3.7 all-to-all-done
  23.9 0.1 copy.17
  23.9 0.2 multiply_reduce_fusion
  24.1 0.1 eq.111
  24.2 0.2 select_reduce_fusion.2
  24.4 0.6 compare_select_fusion.2
  25.0 4.0 %all-gather.2.cloned.1.call-done = bf16[4096,128]{1,0:T(8,128)(2,1)} async-done(((bf16[1024,128]{1,0:T(8,128)(2,1)}), bf16[4096,128]{1,0:T(8,128)(2,1)}) %all-gather.2.cloned.1.call-update) | async-done | bytes 1048592 | tf_op jit(solution)/shard_map/all_gather | solution.py:294
  29.0 2.3 copy.18
  31.3 0.0 copy-done.1
  31.3 283.2 %power_step.1 = f32[8,512,128]{2,1,0:T(8,128)} custom-call(s32[48]{0:T(128)} %get-tuple-element.18.order_ref, s32[48]{0:T(128)} %copy-done.1, s32[48]{0:T(128)} %copy-done.2, s32[48]{0:T(128)} %get-tuple-element.26.before_ref, s32[48]{0:T(128)} %get-tuple-element.25.final_ref, s32[48]{0:T(128)} %compare_select_fusion.1.row_before_ref, ...), custom_call_target="tpu_custom_call" | custom-call | tf_op jit(solution)/shard_map/power_step/pallas_call | solution.py:137
  314.6 1.6 copy-done
  316.1 38.6 %sum_and_gram.1 = (f32[1024,128]{1,0:T(8,128)S(1)}, f32[128,128]{1,0:T(8,128)S(1)}) custom-call(f32[4,1024,128]{2,1,0:T(8,128)S(1)} %bitcast.32), custom_call_target="tpu_custom_call" | custom-call | tf_op jit(solution)/shard_map/sum_and_gram/pallas_call | solution.py:235
  354.7 0.1 copy.19
  354.8 11.7 %cholesky.16 = f32[128,128]{1,0:T(8,128)S(1)} custom-call(f32[128,128]{1,0:T(8,128)S(1)} %fusion.2), custom_call_target="Cholesky" | custom-call | tf_op jit(solution)/shard_map/jit(cholesky)/cholesky | solution.py:304
  366.6 0.6 compare_reduce_fusion
  367.2 0.7 fusion.3
  367.9 0.7 copy.20
  368.6 9.8 %custom-call.6 = f32[1,128,128]{1,2,0:T(8,128)S(1)} custom-call(f32[1,128,128]{2,1,0:T(8,128)S(1)} %get-tuple-element.20), custom_call_target="InvertDiagBlocksLowerTriangular" | custom-call | tf_op jit(solution)/shard_map/triangular_solve | solution.py:305
  378.4 1.4 fusion
  (12 shorter events, 0.1 us)
Async XLA Ops:
  7.2 21.9 %all-gather.2.cloned.1.call-start = ((), (), s32[]{:S(2)}) async-start(), calls=%async_computation.1 | async-start | bytes 1310720 | tf_op jit(solution)/shard_map/all_gather | solution.py:294
  10.2 13.6 %all-to-all-start = ((s32[8,1,6]{2,1,0:T(1,128)}), s32[8,1,6]{2,1,0:T(1,128)S(1)}, u32[]{:S(2)}, u32[]{:S(2)}) async-start(s32[8,1,6]{2,1,0:T(1,128)} %bitcast.5), calls=%async_computation | async-start | bytes 8192 | tf_op jit(solution)/shard_map/all_to_all | solution.py:283
  18.8 12.5 %copy-start.1 = (s32[48]{0:T(128)}, s32[48]{0:T(128)S(1)}, u32[]{:S(2)}) copy-start(s32[48]{0:T(128)S(1)} %get-tuple-element.17.row_ref) | copy-start | bytes 580
  18.8 12.5 %copy-start.2 = (s32[48]{0:T(128)}, s32[48]{0:T(128)S(1)}, u32[]{:S(2)}) copy-start(s32[48]{0:T(128)S(1)} %get-tuple-element.16.live_ref) | copy-start | bytes 580
  314.5 1.6 copy-start
Sparse Core Ops, SparseCore 0:
  9.6 19.4 all-gather.1
